TPU v7x, 32 devices: a whole 2x2x4 slice. The times are simulated.
32 devices in a mesh: shot: 2 (over x), dom: 16 (over z, y, core).
Axes of the slice: x: 2, y: 2, z: 4, core: 2. Of those that a mesh axis runs over, the one named last changes fastest.
Arguments:
- fwd_state: float32 [2, 9, 128, 16, 128], P('shot', None, 'dom'), may hold values from -6 to 6
- adj_state: float32 [2, 9, 128, 16, 128], P('shot', None, 'dom'), may hold values from -6 to 6
- stiff_normal: float32 [3, 128, 16, 128], P(None, 'dom'), may hold values from 0.18 to 0.3
- stiff_coupling: float32 [3, 128, 16, 128], P(None, 'dom'), may hold values from 0.03 to 0.08
- stiff_shear: float32 [3, 128, 16, 128], P(None, 'dom'), may hold values from 0.05 to 0.15
- buoyancy: float32 [128, 16, 128], P('dom'), may hold values from 0.25 to 0.5
- wavelet: float32 [2, 3], P('shot'), may hold values from -16 to 16
- residual: float32 [2, 3, 256], P('shot'), may hold values from -16 to 16
- source_cell: int32 [2], P('shot'), may hold values from 0 to 262143
- receiver_cell: int32 [2, 256], P('shot'), may hold values from 0 to 262143
Outputs:
- gradient: float32 [10, 128, 16, 128], P(None, 'dom', 'shot')
All inputs are finite; a program needn't handle non-finite values.
Results may differ from a plain program's by a relative error of at most 0.00002.
Values sent between devices are 32-bit elements; how exact they have to be, the bound alone decides.
A program may use at most 64 MiB of HBM per device.

v0:
```python
import jax
import jax.numpy as jnp
from jax import lax
from jax.sharding import PartitionSpec as P

ITERS = 3


stencil_taps = (1225.0 / 1024.0, -245.0 / 3072.0, 49.0 / 5120.0, -5.0 / 7168.0)


def padded_2(cells, sides, width):
    for axis, dim in sides:
        count = lax.axis_size(axis)
        ends = count - 1
        head = lax.slice_in_dim(cells, 0, width, axis=dim)
        tail = lax.slice_in_dim(cells, cells.shape[dim] - width, cells.shape[dim], axis=dim)
        cells = jnp.concatenate(
            [
                lax.ppermute(tail, axis, [(i, (i + 1) % count) for i in range(ends)]),
                cells,
                lax.ppermute(head, axis, [((i + 1) % count, i) for i in range(ends)]),
            ],
            axis=dim,
        )
    return cells


def derive(padded, axis_dim, margin, region_start, region_count, forward):
    result = jnp.zeros_like(lax.slice_in_dim(padded, 0, region_count, axis=axis_dim))
    for number in range(4):
        if forward:
            upper_at = margin + region_start + number + 1
            lower_at = margin + region_start - number
        else:
            upper_at = margin + region_start + number
            lower_at = margin + region_start - number - 1
        upper_part = lax.slice_in_dim(padded, upper_at, upper_at + region_count, axis=axis_dim)
        lower_part = lax.slice_in_dim(padded, lower_at, lower_at + region_count, axis=axis_dim)
        result = result + stencil_taps[number] * (upper_part - lower_part)
    return result


def along_axis(source, axis_dim, forward):
    widths = [(0, 0)] * source.ndim
    widths[axis_dim] = (4, 4)
    padded = jnp.pad(source, widths)
    return derive(padded, axis_dim, 4, 0, source.shape[axis_dim], forward)


def strain_set(padded_velocity, margin, region_start, region_count):
    shifted = [padded_velocity[:, :, number] for number in range(3)]
    central = lax.slice_in_dim(
        padded_velocity, margin + region_start, margin + region_start + region_count, axis=3
    )
    middle = [central[:, :, number] for number in range(3)]
    strain_xx = derive(shifted[0], 2, margin, region_start, region_count, False)
    strain_yy = along_axis(middle[1], 3, False)
    strain_zz = along_axis(middle[2], 4, False)
    strain_yz = along_axis(middle[1], 4, True) + along_axis(middle[2], 3, True)
    strain_xz = along_axis(middle[0], 4, True) + derive(
        shifted[2], 2, margin, region_start, region_count, True
    )
    strain_xy = along_axis(middle[0], 3, True) + derive(
        shifted[1], 2, margin, region_start, region_count, True
    )
    return [strain_xx, strain_yy, strain_zz, strain_yz, strain_xz, strain_xy]


def imaging(rebuilt, adjoint):
    return jnp.stack(
        [
            rebuilt[0] * adjoint[0],
            rebuilt[1] * adjoint[1],
            rebuilt[2] * adjoint[2],
            rebuilt[0] * adjoint[1] + rebuilt[1] * adjoint[0],
            rebuilt[0] * adjoint[2] + rebuilt[2] * adjoint[0],
            rebuilt[1] * adjoint[2] + rebuilt[2] * adjoint[1],
            rebuilt[3] * adjoint[3],
            rebuilt[4] * adjoint[4],
            rebuilt[5] * adjoint[5],
            rebuilt[6] * adjoint[6] + rebuilt[7] * adjoint[7] + rebuilt[8] * adjoint[8],
        ]
    )


def stress_update(stresses, strains, moduli, time_sign):
    return [
        stresses[0]
        + time_sign * (moduli[0] * strains[0] + moduli[3] * strains[1] + moduli[4] * strains[2]),
        stresses[1]
        + time_sign * (moduli[3] * strains[0] + moduli[1] * strains[1] + moduli[5] * strains[2]),
        stresses[2]
        + time_sign * (moduli[4] * strains[0] + moduli[5] * strains[1] + moduli[2] * strains[2]),
        stresses[3] + time_sign * (moduli[6] * strains[3]),
        stresses[4] + time_sign * (moduli[7] * strains[4]),
        stresses[5] + time_sign * (moduli[8] * strains[5]),
    ]


def velocity_update(velocity, padded_stress, margin, time_sign, buoyancy):
    cells_x = velocity[0].shape[2]
    shifted = [padded_stress[:, :, number] for number in range(6)]
    central = lax.slice_in_dim(padded_stress, margin, margin + cells_x, axis=3)
    middle = [central[:, :, number] for number in range(6)]
    scaled = time_sign * buoyancy
    return [
        velocity[0]
        + scaled
        * (
            derive(shifted[0], 2, margin, 0, cells_x, True)
            + along_axis(middle[5], 3, False)
            + along_axis(middle[4], 4, False)
        ),
        velocity[1]
        + scaled
        * (
            derive(shifted[5], 2, margin, 0, cells_x, False)
            + along_axis(middle[1], 3, True)
            + along_axis(middle[3], 4, False)
        ),
        velocity[2]
        + scaled
        * (
            derive(shifted[4], 2, margin, 0, cells_x, False)
            + along_axis(middle[3], 3, False)
            + along_axis(middle[2], 4, True)
        ),
    ]


def inject(source, cells_at, values, first_row):
    shot_count, row_count, cells_y, cells_z = source.shape
    volume = row_count * cells_y * cells_z
    local_at = cells_at - first_row * (cells_y * cells_z)
    inside = (local_at >= 0) & (local_at < volume)
    shot_ids = lax.broadcasted_iota(jnp.int32, cells_at.shape, 0)
    flattened = (
        source.reshape(shot_count, volume)
        .at[shot_ids, jnp.where(inside, local_at, 0)]
        .add(jnp.where(inside, values, jnp.zeros_like(values)))
    )
    return flattened.reshape(source.shape)


def body(
    fwd_state,
    adj_state,
    stiff_normal,
    stiff_coupling,
    stiff_shear,
    buoyancy,
    wavelet,
    residual,
    source_cell,
    receiver_cell,
):
    cells_x = fwd_state.shape[2]
    time_sign = jnp.array([-1.0, 1.0], jnp.float32).reshape(1, 2, 1, 1, 1)
    anchor = lax.axis_index("dom") * cells_x
    paired = jnp.stack([fwd_state, adj_state], axis=1)
    velocity_all = paired[:, :, 0:3]
    stress_all = paired[:, :, 3:9]
    stiffness = jnp.concatenate([stiff_normal, stiff_coupling, stiff_shear], axis=0)
    running = jnp.zeros((10,) + buoyancy.shape, jnp.float32)
    for step_index in range(ITERS):
        velocity = [velocity_all[:, :, number] for number in range(3)]
        padded_velocity = padded_2(velocity_all, (("dom", 3),), 4)
        strains = strain_set(padded_velocity, 4, 0, cells_x)
        stresses = stress_update(
            [stress_all[:, :, number] for number in range(6)],
            strains,
            [stiffness[number] for number in range(9)],
            time_sign,
        )
        factors = strains + velocity
        running = running + jnp.sum(
            imaging([item[:, 0] for item in factors], [item[:, 1] for item in factors]), axis=1
        )
        source_values = -wavelet[:, step_index : step_index + 1]
        for number in range(3):
            stresses[number] = (
                stresses[number]
                .at[:, 0]
                .set(inject(stresses[number][:, 0], source_cell[:, None], source_values, anchor))
            )
        stress_stack = jnp.stack(stresses, axis=2)
        padded_stress = padded_2(stress_stack, (("dom", 3),), 4)
        stress_all = stress_stack
        velocity = velocity_update(velocity, padded_stress, 4, time_sign, buoyancy)
        velocity[2] = (
            velocity[2]
            .at[:, 1]
            .set(inject(velocity[2][:, 1], receiver_cell, residual[:, step_index], anchor))
        )
        velocity_all = jnp.stack(velocity, axis=2)
    gradient = lax.psum_scatter(running, "shot", scatter_dimension=2, tiled=True)
    return gradient / ITERS


def solution(mesh):
    placed = (
        P("shot", None, "dom", None, None),
        P("shot", None, "dom", None, None),
        P(None, "dom", None, None),
        P(None, "dom", None, None),
        P(None, "dom", None, None),
        P("dom", None, None),
        P("shot", None),
        P("shot", None, None),
        P("shot"),
        P("shot", None),
    )
    return jax.shard_map(
        body, mesh=mesh, in_specs=placed, out_specs=P(None, "dom", "shot", None), check_vma=False
    )
```

profile of v0, /device:TPU:9, one launch (start us, length us, event | category | flops | bytes accessed | tf_op | source)
XLA Modules:
  0.0 126.8 jit_solution(9082591278316164754)
XLA Ops:
  6.5 1.2 fusion.4
  7.7 3.7 %collective-permute-start = (f32[1,2,3,4,16,128]{5,4,3,1,2,0:T(8,128)S(1)}, f32[1,2,3,4,16,128]{5,4,3,1,2,0:T(8,128)S(1)}, u32[]{:S(2)}, u32[]{:S(2)}) collective-permute-start(f32[1,2,3,4,16,128]{5,4,3,1,2,0:T(8,128)S(1)} %get-tuple-element.209), channel_id=1, source_target_pairs={{0,1},{1,2},{2,3},{3,4},{4,5},{5,6},{6,7},{7,8},{8,9},{9,10},{10,1... | collective-permute-start | bytes 589832 | tf_op jit(solution)/shard_map/ppermute | solution.py:20
  11.4 1.9 %collective-permute-start.1 = (f32[1,2,3,4,16,128]{5,4,3,1,2,0:T(8,128)S(1)}, f32[1,2,3,4,16,128]{5,4,3,1,2,0:T(8,128)S(1)}, u32[]{:S(2)}, u32[]{:S(2)}) collective-permute-start(f32[1,2,3,4,16,128]{5,4,3,1,2,0:T(8,128)S(1)} %get-tuple-element.210), channel_id=1, source_target_pairs={{1,0},{2,1},{3,2},{4,3},{5,4},{6,5},{7,6},{8,7},{9,8},{10,9},{11,1... | collective-permute-start | bytes 589832 | tf_op jit(solution)/shard_map/ppermute | solution.py:22
  14.2 0.6 copy-done.19
  14.8 0.6 fusion.360
  16.8 0.7 slice_bitcast_fusion.9
  17.5 0.7 and_reduce_fusion
  18.2 0.2 collective-permute-done.1
  18.6 0.6 copy-done.18
  19.1 0.3 fusion.313
  19.5 0.6 constant_dynamic-update-slice_fusion.9
  20.2 0.7 fusion.362
  20.9 0.7 fusion.363
  25.5 0.7 fusion.361
  28.1 0.6 constant_dynamic-update-slice_fusion.8
  28.8 0.6 constant_dynamic-update-slice_fusion.7
  29.4 0.6 constant_dynamic-update-slice_fusion.6
  30.0 0.7 constant_dynamic-update-slice_fusion.5
  30.7 0.6 constant_dynamic-update-slice_fusion.4
  31.4 0.3 bitcast_dynamic-update-slice_fusion.7
  31.7 0.5 copy-done.13
  32.2 0.3 bitcast_dynamic-update-slice_fusion.6
  32.6 0.5 copy-done.11
  33.1 0.2 bitcast_dynamic-update-slice_fusion.5
  33.3 3.6 %collective-permute-start.2 = (f32[1,2,6,4,16,128]{5,4,3,1,2,0:T(8,128)S(1)}, f32[1,2,6,4,16,128]{5,4,3,1,2,0:T(8,128)S(1)}, u32[]{:S(2)}, u32[]{:S(2)}) collective-permute-start(f32[1,2,6,4,16,128]{5,4,3,1,2,0:T(8,128)S(1)} %get-tuple-element.219), channel_id=1, source_target_pairs={{0,1},{1,2},{2,3},{3,4},{4,5},{5,6},{6,7},{7,8},{8,9},{9,10},{10,1... | collective-permute-start | bytes 1179656 | tf_op jit(solution)/shard_map/ppermute | solution.py:20
  36.9 1.9 %collective-permute-start.3 = (f32[1,2,6,4,16,128]{5,4,3,1,2,0:T(8,128)S(1)}, f32[1,2,6,4,16,128]{5,4,3,1,2,0:T(8,128)S(1)}, u32[]{:S(2)}, u32[]{:S(2)}) collective-permute-start(f32[1,2,6,4,16,128]{5,4,3,1,2,0:T(8,128)S(1)} %get-tuple-element.220), channel_id=1, source_target_pairs={{1,0},{2,1},{3,2},{4,3},{5,4},{6,5},{7,6},{8,7},{9,8},{10,9},{11,1... | collective-permute-start | bytes 1179656 | tf_op jit(solution)/shard_map/ppermute | solution.py:22
  38.9 2.7 %collective-permute-done.2 = f32[1,2,6,4,16,128]{5,4,3,1,2,0:T(8,128)S(1)} collective-permute-done((f32[1,2,6,4,16,128]{5,4,3,1,2,0:T(8,128)S(1)}, f32[1,2,6,4,16,128]{5,4,3,1,2,0:T(8,128)S(1)}, u32[]{:S(2)}, u32[]{:S(2)}) %collective-permute-start.2) | collective-permute-done | bytes 393248 | tf_op jit(solution)/shard_map/ppermute | solution.py:20
  41.6 6.7 %collective-permute-done.3 = f32[1,2,6,4,16,128]{5,4,3,1,2,0:T(8,128)S(1)} collective-permute-done((f32[1,2,6,4,16,128]{5,4,3,1,2,0:T(8,128)S(1)}, f32[1,2,6,4,16,128]{5,4,3,1,2,0:T(8,128)S(1)}, u32[]{:S(2)}, u32[]{:S(2)}) %collective-permute-start.3) | collective-permute-done | bytes 393248 | tf_op jit(solution)/shard_map/ppermute | solution.py:22
  48.4 0.3 fusion.82
  48.7 0.3 fusion.81
  49.0 2.3 %scatter_fusion = f32[16384]{0:T(1024)S(1)} fusion(f32[16384]{0:T(1024)S(1)} %bitcast.1032, s32[256]{0:T(256)S(1)} %bitcast.1072, f32[256]{0:T(256)S(1)} %bitcast.1075), kind=kCustom, calls=%fused_computation | custom fusion | flops 256 | bytes 4096 | tf_op jit(solution)/shard_map/scatter-add | solution.py:141
  51.4 0.3 fusion.80
  51.8 1.9 %collective-permute-start.4 = (f32[1,2,3,4,16,128]{5,4,3,1,2,0:T(8,128)S(1)}, f32[1,2,3,4,16,128]{5,4,3,1,2,0:T(8,128)S(1)}, u32[]{:S(2)}, u32[]{:S(2)}) collective-permute-start(f32[1,2,3,4,16,128]{5,4,3,1,2,0:T(8,128)S(1)} %get-tuple-element.228), channel_id=1, source_target_pairs={{0,1},{1,2},{2,3},{3,4},{4,5},{5,6},{6,7},{7,8},{8,9},{9,10},{10,1... | collective-permute-start | bytes 589832 | tf_op jit(solution)/shard_map/ppermute | solution.py:20
  53.7 2.4 %collective-permute-start.5 = (f32[1,2,3,4,16,128]{5,4,3,1,2,0:T(8,128)S(1)}, f32[1,2,3,4,16,128]{5,4,3,1,2,0:T(8,128)S(1)}, u32[]{:S(2)}, u32[]{:S(2)}) collective-permute-start(f32[1,2,3,4,16,128]{5,4,3,1,2,0:T(8,128)S(1)} %get-tuple-element.229), channel_id=1, source_target_pairs={{1,0},{2,1},{3,2},{4,3},{5,4},{6,5},{7,6},{8,7},{9,8},{10,9},{11,1... | collective-permute-start | bytes 589832 | tf_op jit(solution)/shard_map/ppermute | solution.py:22
  56.3 4.4 %collective-permute-done.5 = f32[1,2,3,4,16,128]{5,4,3,1,2,0:T(8,128)S(1)} collective-permute-done((f32[1,2,3,4,16,128]{5,4,3,1,2,0:T(8,128)S(1)}, f32[1,2,3,4,16,128]{5,4,3,1,2,0:T(8,128)S(1)}, u32[]{:S(2)}, u32[]{:S(2)}) %collective-permute-start.5) | collective-permute-done | bytes 196640 | tf_op jit(solution)/shard_map/ppermute | solution.py:22
  60.8 0.8 copy-done.10
  61.6 0.3 multiply_add_fusion.4
  61.9 0.6 constant_dynamic-update-slice_fusion.19
  62.6 0.7 fusion.366
  65.2 0.7 fusion.364
  67.8 0.7 fusion.365
  70.4 0.3 bitcast_dynamic-update-slice_fusion.2
  70.8 0.7 copy-done.3
  71.6 0.7 copy-done.14
  72.3 0.3 bitcast_dynamic-update-slice_fusion.1
  72.6 0.5 copy-done.12
  73.4 1.9 %collective-permute-start.6 = (f32[1,2,6,4,16,128]{5,4,3,1,2,0:T(8,128)S(1)}, f32[1,2,6,4,16,128]{5,4,3,1,2,0:T(8,128)S(1)}, u32[]{:S(2)}, u32[]{:S(2)}) collective-permute-start(f32[1,2,6,4,16,128]{5,4,3,1,2,0:T(8,128)S(1)} %get-tuple-element.214), channel_id=1, source_target_pairs={{0,1},{1,2},{2,3},{3,4},{4,5},{5,6},{6,7},{7,8},{8,9},{9,10},{10,1... | collective-permute-start | bytes 1179656 | tf_op jit(solution)/shard_map/ppermute | solution.py:20
  75.3 2.4 %collective-permute-start.7 = (f32[1,2,6,4,16,128]{5,4,3,1,2,0:T(8,128)S(1)}, f32[1,2,6,4,16,128]{5,4,3,1,2,0:T(8,128)S(1)}, u32[]{:S(2)}, u32[]{:S(2)}) collective-permute-start(f32[1,2,6,4,16,128]{5,4,3,1,2,0:T(8,128)S(1)} %get-tuple-element.215), channel_id=1, source_target_pairs={{1,0},{2,1},{3,2},{4,3},{5,4},{6,5},{7,6},{8,7},{9,8},{10,9},{11,1... | collective-permute-start | bytes 1179656 | tf_op jit(solution)/shard_map/ppermute | solution.py:22
  77.8 2.2 %collective-permute-done.6 = f32[1,2,6,4,16,128]{5,4,3,1,2,0:T(8,128)S(1)} collective-permute-done((f32[1,2,6,4,16,128]{5,4,3,1,2,0:T(8,128)S(1)}, f32[1,2,6,4,16,128]{5,4,3,1,2,0:T(8,128)S(1)}, u32[]{:S(2)}, u32[]{:S(2)}) %collective-permute-start.6) | collective-permute-done | bytes 393248 | tf_op jit(solution)/shard_map/ppermute | solution.py:20
  80.0 6.2 %collective-permute-done.7 = f32[1,2,6,4,16,128]{5,4,3,1,2,0:T(8,128)S(1)} collective-permute-done((f32[1,2,6,4,16,128]{5,4,3,1,2,0:T(8,128)S(1)}, f32[1,2,6,4,16,128]{5,4,3,1,2,0:T(8,128)S(1)}, u32[]{:S(2)}, u32[]{:S(2)}) %collective-permute-start.7) | collective-permute-done | bytes 393248 | tf_op jit(solution)/shard_map/ppermute | solution.py:22
  86.2 0.3 fusion.83
  86.7 0.3 fusion.84
  87.1 0.3 fusion.85
  87.5 2.3 %scatter_fusion.1 = f32[16384]{0:T(1024)S(1)} fusion(f32[16384]{0:T(1024)S(1)} %bitcast.1029, s32[256]{0:T(256)S(1)} %bitcast.1073, f32[256]{0:T(256)S(1)} %bitcast.1074), kind=kCustom, calls=%fused_computation.1 | custom fusion | flops 256 | bytes 4096 | tf_op jit(solution)/shard_map/scatter-add | solution.py:141
  89.9 0.3 fusion.63
  90.2 1.9 %collective-permute-start.8 = (f32[1,2,3,4,16,128]{5,4,3,1,2,0:T(8,128)S(1)}, f32[1,2,3,4,16,128]{5,4,3,1,2,0:T(8,128)S(1)}, u32[]{:S(2)}, u32[]{:S(2)}) collective-permute-start(f32[1,2,3,4,16,128]{5,4,3,1,2,0:T(8,128)S(1)} %get-tuple-element.226), channel_id=1, source_target_pairs={{0,1},{1,2},{2,3},{3,4},{4,5},{5,6},{6,7},{7,8},{8,9},{9,10},{10,1... | collective-permute-start | bytes 589832 | tf_op jit(solution)/shard_map/ppermute | solution.py:20
  92.2 2.4 %collective-permute-start.9 = (f32[1,2,3,4,16,128]{5,4,3,1,2,0:T(8,128)S(1)}, f32[1,2,3,4,16,128]{5,4,3,1,2,0:T(8,128)S(1)}, u32[]{:S(2)}, u32[]{:S(2)}) collective-permute-start(f32[1,2,3,4,16,128]{5,4,3,1,2,0:T(8,128)S(1)} %get-tuple-element.227), channel_id=1, source_target_pairs={{1,0},{2,1},{3,2},{4,3},{5,4},{6,5},{7,6},{8,7},{9,8},{10,9},{11,1... | collective-permute-start | bytes 589832 | tf_op jit(solution)/shard_map/ppermute | solution.py:22
  94.6 0.3 fusion.250
  94.9 4.3 %collective-permute-done.9 = f32[1,2,3,4,16,128]{5,4,3,1,2,0:T(8,128)S(1)} collective-permute-done((f32[1,2,3,4,16,128]{5,4,3,1,2,0:T(8,128)S(1)}, f32[1,2,3,4,16,128]{5,4,3,1,2,0:T(8,128)S(1)}, u32[]{:S(2)}, u32[]{:S(2)}) %collective-permute-start.9) | collective-permute-done | bytes 196640 | tf_op jit(solution)/shard_map/ppermute | solution.py:22
  99.5 0.3 fusion.150
  100.0 1.0 copy-done.5
  101.0 1.0 fusion
  102.0 16.2 %reduce-scatter.2.cloned.1.call-done = f32[10,8,8,128]{3,2,1,0:T(8,128)} async-done(((f32[10,8,16,128]{3,2,1,0:T(8,128)}), f32[10,8,8,128]{3,2,1,0:T(8,128)}) %reduce-scatter.2.cloned.1.call-update) | async-done | bytes 327696 | tf_op jit(solution)/shard_map/reduce_scatter | solution.py:197
  118.3 1.7 %broadcast_multiply_fusion = f32[10,8,8,128]{3,2,1,0:T(8,128)} fusion(f32[10,8,8,128]{3,2,1,0:T(8,128)} %reduce-scatter.2.cloned.1.call-done), kind=kLoop, calls=%fused_computation.432 | loop fusion | flops 81920 | bytes 655360 | tf_op jit(solution)/shard_map/div | solution.py:198
  (119 shorter events, 2.6 us)
Async XLA Ops:
  6.5 111.7 %reduce-scatter.2.cloned.1.call-start = ((), (), s32[]{:S(2)}) async-start(), calls=%async_computation.1 | async-start | bytes 983040 | tf_op jit(solution)/shard_map/reduce_scatter | solution.py:197
  6.5 7.5 %copy-start = (f32[1,9,8,16,128]{4,3,2,1,0:T(8,128)S(1)}, f32[1,9,8,16,128]{4,3,2,1,0:T(8,128)}, u32[]{:S(2)}) copy-start(f32[1,9,8,16,128]{4,3,2,1,0:T(8,128)} %param.39) | copy-start | bytes 1769476
  6.5 7.5 %copy-start.1 = (f32[1,9,8,16,128]{4,3,2,1,0:T(8,128)S(1)}, f32[1,9,8,16,128]{4,3,2,1,0:T(8,128)}, u32[]{:S(2)}) copy-start(f32[1,9,8,16,128]{4,3,2,1,0:T(8,128)} %param.40) | copy-start | bytes 1769476
  7.7 10.5 %collective-permute-start = (f32[1,2,3,4,16,128]{5,4,3,1,2,0:T(8,128)S(1)}, f32[1,2,3,4,16,128]{5,4,3,1,2,0:T(8,128)S(1)}, u32[]{:S(2)}, u32[]{:S(2)}) collective-permute-start(f32[1,2,3,4,16,128]{5,4,3,1,2,0:T(8,128)S(1)} %get-tuple-element.209), channel_id=1, source_target_pairs={{0,1},{1,2},{2,3},{3,4},{4,5},{5,6},{6,7},{7,8},{8,9},{9,10},{10,1... | collective-permute-start | bytes 589832 | tf_op jit(solution)/shard_map/ppermute | solution.py:20
  11.4 7.0 %collective-permute-start.1 = (f32[1,2,3,4,16,128]{5,4,3,1,2,0:T(8,128)S(1)}, f32[1,2,3,4,16,128]{5,4,3,1,2,0:T(8,128)S(1)}, u32[]{:S(2)}, u32[]{:S(2)}) collective-permute-start(f32[1,2,3,4,16,128]{5,4,3,1,2,0:T(8,128)S(1)} %get-tuple-element.210), channel_id=1, source_target_pairs={{1,0},{2,1},{3,2},{4,3},{5,4},{6,5},{7,6},{8,7},{9,8},{10,9},{11,1... | collective-permute-start | bytes 589832 | tf_op jit(solution)/shard_map/ppermute | solution.py:22
  14.1 0.7 copy-start.19
  14.1 0.7 copy-start.20
  14.1 2.6 %copy-start.21 = (f32[1,3,256]{2,0,1:T(1,128)S(1)}, f32[1,3,256]{2,0,1:T(1,128)}, u32[]{:S(2)}) copy-start(f32[1,3,256]{2,0,1:T(1,128)} %param.46) | copy-start | bytes 9220
  14.1 2.6 %copy-start.15 = (f32[3,8,16,128]{3,2,1,0:T(8,128)S(1)}, f32[3,8,16,128]{3,2,1,0:T(8,128)}, u32[]{:S(2)}) copy-start(f32[3,8,16,128]{3,2,1,0:T(8,128)} %param.41) | copy-start | bytes 589828
  14.1 2.6 %copy-start.16 = (f32[3,8,16,128]{3,2,1,0:T(8,128)S(1)}, f32[3,8,16,128]{3,2,1,0:T(8,128)}, u32[]{:S(2)}) copy-start(f32[3,8,16,128]{3,2,1,0:T(8,128)} %param.42) | copy-start | bytes 589828
  14.8 2.0 %copy-start.17 = (f32[3,8,16,128]{3,2,1,0:T(8,128)S(1)}, f32[3,8,16,128]{3,2,1,0:T(8,128)}, u32[]{:S(2)}) copy-start(f32[3,8,16,128]{3,2,1,0:T(8,128)} %param.43) | copy-start | bytes 589828
  16.8 1.8 %copy-start.9 = (f32[8,16,128]{2,1,0:T(8,128)}, f32[8,16,128]{2,1,0:T(8,128)S(1)}, u32[]{:S(2)}) copy-start(f32[8,16,128]{2,1,0:T(8,128)S(1)} %get-tuple-element.235) | copy-start | bytes 196612
  16.8 3.3 %copy-start.7 = (f32[8,16,128]{2,1,0:T(8,128)}, f32[8,16,128]{2,1,0:T(8,128)S(1)}, u32[]{:S(2)}) copy-start(f32[8,16,128]{2,1,0:T(8,128)S(1)} %get-tuple-element.236) | copy-start | bytes 196612
  18.5 0.7 copy-start.18
  31.4 0.8 copy-start.13
  32.2 0.8 copy-start.11
  33.3 5.6 %copy-start.6 = (f32[10,1,8,16,128]{4,3,2,1,0:T(8,128)S(1)}, f32[10,1,8,16,128]{4,3,2,1,0:T(8,128)}, u32[]{:S(2)}) copy-start(f32[10,1,8,16,128]{4,3,2,1,0:T(8,128)} %get-tuple-element.257) | copy-start | bytes 1966084
  33.3 8.3 %collective-permute-start.2 = (f32[1,2,6,4,16,128]{5,4,3,1,2,0:T(8,128)S(1)}, f32[1,2,6,4,16,128]{5,4,3,1,2,0:T(8,128)S(1)}, u32[]{:S(2)}, u32[]{:S(2)}) collective-permute-start(f32[1,2,6,4,16,128]{5,4,3,1,2,0:T(8,128)S(1)} %get-tuple-element.219), channel_id=1, source_target_pairs={{0,1},{1,2},{2,3},{3,4},{4,5},{5,6},{6,7},{7,8},{8,9},{9,10},{10,1... | collective-permute-start | bytes 1179656 | tf_op jit(solution)/shard_map/ppermute | solution.py:20
  36.9 11.4 %collective-permute-start.3 = (f32[1,2,6,4,16,128]{5,4,3,1,2,0:T(8,128)S(1)}, f32[1,2,6,4,16,128]{5,4,3,1,2,0:T(8,128)S(1)}, u32[]{:S(2)}, u32[]{:S(2)}) collective-permute-start(f32[1,2,6,4,16,128]{5,4,3,1,2,0:T(8,128)S(1)} %get-tuple-element.220), channel_id=1, source_target_pairs={{1,0},{2,1},{3,2},{4,3},{5,4},{6,5},{7,6},{8,7},{9,8},{10,9},{11,1... | collective-permute-start | bytes 1179656 | tf_op jit(solution)/shard_map/ppermute | solution.py:22
  38.9 9.4 %copy-start.2 = (f32[8,16,128]{2,1,0:T(8,128)S(1)}, f32[8,16,128]{2,1,0:T(8,128)}, u32[]{:S(2)}) copy-start(f32[8,16,128]{2,1,0:T(8,128)} %param.44) | copy-start | bytes 196612
  51.8 4.5 %collective-permute-start.4 = (f32[1,2,3,4,16,128]{5,4,3,1,2,0:T(8,128)S(1)}, f32[1,2,3,4,16,128]{5,4,3,1,2,0:T(8,128)S(1)}, u32[]{:S(2)}, u32[]{:S(2)}) collective-permute-start(f32[1,2,3,4,16,128]{5,4,3,1,2,0:T(8,128)S(1)} %get-tuple-element.228), channel_id=1, source_target_pairs={{0,1},{1,2},{2,3},{3,4},{4,5},{5,6},{6,7},{7,8},{8,9},{9,10},{10,1... | collective-permute-start | bytes 589832 | tf_op jit(solution)/shard_map/ppermute | solution.py:20
  53.7 7.0 %collective-permute-start.5 = (f32[1,2,3,4,16,128]{5,4,3,1,2,0:T(8,128)S(1)}, f32[1,2,3,4,16,128]{5,4,3,1,2,0:T(8,128)S(1)}, u32[]{:S(2)}, u32[]{:S(2)}) collective-permute-start(f32[1,2,3,4,16,128]{5,4,3,1,2,0:T(8,128)S(1)} %get-tuple-element.229), channel_id=1, source_target_pairs={{1,0},{2,1},{3,2},{4,3},{5,4},{6,5},{7,6},{8,7},{9,8},{10,9},{11,1... | collective-permute-start | bytes 589832 | tf_op jit(solution)/shard_map/ppermute | solution.py:22
  60.7 0.8 copy-start.10
  61.6 1.0 copy-start.8
  70.4 1.1 copy-start.3
  71.5 0.8 copy-start.14
  72.3 0.8 copy-start.12
  73.4 6.6 %collective-permute-start.6 = (f32[1,2,6,4,16,128]{5,4,3,1,2,0:T(8,128)S(1)}, f32[1,2,6,4,16,128]{5,4,3,1,2,0:T(8,128)S(1)}, u32[]{:S(2)}, u32[]{:S(2)}) collective-permute-start(f32[1,2,6,4,16,128]{5,4,3,1,2,0:T(8,128)S(1)} %get-tuple-element.214), channel_id=1, source_target_pairs={{0,1},{1,2},{2,3},{3,4},{4,5},{5,6},{6,7},{7,8},{8,9},{9,10},{10,1... | collective-permute-start | bytes 1179656 | tf_op jit(solution)/shard_map/ppermute | solution.py:20
  75.3 10.9 %collective-permute-start.7 = (f32[1,2,6,4,16,128]{5,4,3,1,2,0:T(8,128)S(1)}, f32[1,2,6,4,16,128]{5,4,3,1,2,0:T(8,128)S(1)}, u32[]{:S(2)}, u32[]{:S(2)}) collective-permute-start(f32[1,2,6,4,16,128]{5,4,3,1,2,0:T(8,128)S(1)} %get-tuple-element.215), channel_id=1, source_target_pairs={{1,0},{2,1},{3,2},{4,3},{5,4},{6,5},{7,6},{8,7},{9,8},{10,9},{11,1... | collective-permute-start | bytes 1179656 | tf_op jit(solution)/shard_map/ppermute | solution.py:22
  77.8 8.4 %copy-start.4 = (f32[10,1,8,16,128]{4,3,2,1,0:T(8,128)}, f32[10,1,8,16,128]{4,3,2,1,0:T(8,128)S(1)}, u32[]{:S(2)}) copy-start(f32[10,1,8,16,128]{4,3,2,1,0:T(8,128)S(1)} %constant_dynamic-update-slice_fusion.10) | copy-start | bytes 1966084
  90.2 4.7 %collective-permute-start.8 = (f32[1,2,3,4,16,128]{5,4,3,1,2,0:T(8,128)S(1)}, f32[1,2,3,4,16,128]{5,4,3,1,2,0:T(8,128)S(1)}, u32[]{:S(2)}, u32[]{:S(2)}) collective-permute-start(f32[1,2,3,4,16,128]{5,4,3,1,2,0:T(8,128)S(1)} %get-tuple-element.226), channel_id=1, source_target_pairs={{0,1},{1,2},{2,3},{3,4},{4,5},{5,6},{6,7},{7,8},{8,9},{9,10},{10,1... | collective-permute-start | bytes 589832 | tf_op jit(solution)/shard_map/ppermute | solution.py:20
  92.2 7.0 %collective-permute-start.9 = (f32[1,2,3,4,16,128]{5,4,3,1,2,0:T(8,128)S(1)}, f32[1,2,3,4,16,128]{5,4,3,1,2,0:T(8,128)S(1)}, u32[]{:S(2)}, u32[]{:S(2)}) collective-permute-start(f32[1,2,3,4,16,128]{5,4,3,1,2,0:T(8,128)S(1)} %get-tuple-element.227), channel_id=1, source_target_pairs={{1,0},{2,1},{3,2},{4,3},{5,4},{6,5},{7,6},{8,7},{9,8},{10,9},{11,1... | collective-permute-start | bytes 589832 | tf_op jit(solution)/shard_map/ppermute | solution.py:22
  99.9 1.1 copy-start.5
Sparse Core Ops, SparseCore 0:
  102.2 16.0 reduce-scatter.1
where the time goes:
time: 129 us; the launch traced here: 127 us
  waiting for transfers between devices  43 us (33%)
  between operations  27.6 us (21%)
  starting transfers between devices  24.1 us (19%)
  other arithmetic  24 us (19%)
  local copies, waits for them, and re-layouts  8.2 us (6%)
    ppermute x5, waiting for transfers between devices, padded_2(): lax.ppermute(head, axis, [((i + 1) % count, i) for i in range(ends)])  21.7 us
    reduce_scatter x1, waiting for transfers between devices, body(): lax.psum_scatter(running, 'shot', scatter_dimension=2, tiled=True)  16.2 us
    ppermute x5, starting transfers between devices, padded_2(): lax.ppermute(tail, axis, [(i, (i + 1) % count) for i in range(ends)])  13 us
    ppermute x5, starting transfers between devices, padded_2(): lax.ppermute(head, axis, [((i + 1) % count, i) for i in range(ends)])  11.1 us
    unnamed x50, local copies, waits for them, and re-layouts  6.07 us
    unnamed x31, other arithmetic  5.98 us
    ppermute x5, waiting for transfers between devices, padded_2(): lax.ppermute(tail, axis, [(i, (i + 1) % count) for i in range(ends)])  5.03 us
    scatter-add x2, other arithmetic, inject(): flattened = source.reshape(shot_count, volume).at[shot_ids, jnp.where(ins...  4.62 us
  transfers between devices with their start and end apart: 11, of which 9 were waited for; matrix products, arithmetic and copies ran while one was open for 2% of the time, Pallas kernels for 0%

commit v1 on v0

v1 whole, which is shorter than its diff:
```python
import functools

import jax
import jax.numpy as jnp
from jax import lax
from jax.experimental import pallas as pl
from jax.experimental.pallas import tpu as pltpu
from jax.sharding import PartitionSpec as P

ITERS = 3
TAPS = (1225.0 / 1024.0, -245.0 / 3072.0, 49.0 / 5120.0, -5.0 / 7168.0)
MESH = pl.DeviceIdType.MESH
F32 = jnp.float32
BF16 = jnp.bfloat16

VEL_UP = ((slice(0, 1), 8, 0, 4), (slice(1, 3), 9, 1, 3))
VEL_DOWN = ((slice(0, 1), 4, 12, 3), (slice(1, 3), 4, 12, 4))
STR_UP = ((slice(0, 1), 9, 1, 3), (slice(1, 3), 8, 0, 4))
STR_DOWN = ((slice(0, 1), 4, 12, 4), (slice(1, 3), 4, 12, 3))


def split2(f):
    hi = f.astype(BF16)
    return hi, (f - hi.astype(F32)).astype(BF16)


def band(offset, forward):
    out = jnp.zeros(offset.shape, F32)
    for m in range(1, 5):
        plus, minus = (m, 1 - m) if forward else (m - 1, -m)
        out = jnp.where(offset == plus, F32(TAPS[m - 1]), out)
        out = jnp.where(offset == minus, F32(-TAPS[m - 1]), out)
    return out


def kernel(
    shots, doms, fwd, adj, cn, cc, cs, buoy, wav, res, src, rcv, out,
    V, S, T, C, B, E, Q, RI, GL, GX, RL, RX, MZ, MY,
    load_sem, ssem, rsem, gs_sem, gr_sem,
):
    nx, ny, nz = 8, V.shape[3], V.shape[4]
    rows = nx * ny
    yp = ny // shots
    dom = lax.axis_index("dom")
    shot = lax.axis_index("shot")
    has_lo = dom > 0
    has_hi = dom < doms - 1
    above = lax.rem(dom + 1, doms)
    below = lax.rem(dom + doms - 1, doms)

    loads = []

    def load(a, b):
        c = pltpu.make_async_copy(a, b, load_sem.at[len(loads)])
        c.start()
        loads.append(c)

    states = (fwd, adj)
    for w in range(2):
        load(states[w].at[0, 0:3], V.at[w, :, pl.ds(4, nx)])
    for w in range(2):
        load(states[w].at[0, 3], S.at[w, 0, pl.ds(4, nx)])
        load(states[w].at[0, 8], S.at[w, 1, pl.ds(4, nx)])
        load(states[w].at[0, 7], S.at[w, 2, pl.ds(4, nx)])
        load(states[w].at[0, 4:7], T.at[w])
    load(cn, C.at[0:3])
    load(cc, C.at[3:6])
    load(cs, C.at[6:9])
    load(buoy, B)

    barrier = pltpu.get_barrier_semaphore()

    @pl.when(has_lo)
    def _():
        pl.semaphore_signal(barrier, inc=1, device_id={"dom": below}, device_id_type=MESH)

    @pl.when(has_hi)
    def _():
        pl.semaphore_signal(barrier, inc=1, device_id={"dom": above}, device_id_type=MESH)

    for o in range(1, shots):
        pl.semaphore_signal(
            barrier, inc=1, device_id={"shot": lax.rem(shot + o, shots)}, device_id_type=MESH
        )

    @pl.when(jnp.logical_not(has_lo))
    def _():
        V[:, :, 0:4] = jnp.zeros((2, 3, 4, ny, nz), F32)
        S[:, :, 0:4] = jnp.zeros((2, 3, 4, ny, nz), F32)

    @pl.when(jnp.logical_not(has_hi))
    def _():
        V[:, :, 12:16] = jnp.zeros((2, 3, 4, ny, nz), F32)
        S[:, :, 12:16] = jnp.zeros((2, 3, 4, ny, nz), F32)

    pl.semaphore_wait(
        barrier, has_lo.astype(jnp.int32) + has_hi.astype(jnp.int32) + (shots - 1)
    )

    def message(stage, w, side):
        buf = S if stage % 2 else V
        plan = ((VEL_UP, VEL_DOWN), (STR_UP, STR_DOWN))[stage % 2][side]
        copies = []
        for piece, (comp, at, to, count) in enumerate(plan):
            if stage == 0:
                source = states[w].at[0, comp, pl.ds(at - 4, count)]
            else:
                source = buf.at[w, comp, pl.ds(at, count)]
            copies.append(
                pltpu.make_async_remote_copy(
                    src_ref=source,
                    dst_ref=buf.at[w, comp, pl.ds(to, count)],
                    send_sem=ssem.at[stage, w, side, piece],
                    recv_sem=rsem.at[stage, w, side, piece],
                    device_id={"dom": below if side else above},
                    device_id_type=MESH,
                )
            )
        return copies

    def send(stage, w):
        @pl.when(has_hi)
        def _():
            for c in message(stage, w, 0):
                c.start()

        @pl.when(has_lo)
        def _():
            for c in message(stage, w, 1):
                c.start()

    def wait_send(stage, w):
        @pl.when(has_hi)
        def _():
            for c in message(stage, w, 0):
                c.wait_send()

        @pl.when(has_lo)
        def _():
            for c in message(stage, w, 1):
                c.wait_send()

    def wait_recv(stage, w):
        @pl.when(has_lo)
        def _():
            for c in message(stage, w, 0):
                c.wait_recv()

        @pl.when(has_hi)
        def _():
            for c in message(stage, w, 1):
                c.wait_recv()

    for w in range(2):
        send(0, w)

    r = lax.broadcasted_iota(jnp.int32, (nz, nz), 0)
    c = lax.broadcasted_iota(jnp.int32, (nz, nz), 1)
    for f in range(2):
        hi, mid = split2(band(r - c, f == 1))
        half = jnp.concatenate([hi, mid], axis=1)
        MZ[f] = jnp.concatenate([half, half], axis=0)
    r = lax.broadcasted_iota(jnp.int32, (rows, rows), 0)
    c = lax.broadcasted_iota(jnp.int32, (rows, rows), 1)
    for f in range(2):
        coef = jnp.where(r // ny == c // ny, band(c - r, f == 1), F32(0.0))
        hi, mid = split2(coef)
        half = jnp.concatenate([hi, mid], axis=0)
        MY[f] = jnp.concatenate([half, half], axis=1)

    cell = rcv[...]
    local = cell - dom * (rows * nz)
    cell_row = lax.shift_right_arithmetic(local, 7)
    cell_z = jnp.bitwise_and(local, 127)
    nrec = cell.shape[1]
    at_row = lax.broadcasted_iota(jnp.int32, (rows, nrec), 0) == cell_row
    at_z = (lax.broadcasted_iota(jnp.int32, (nz, nrec), 0) == cell_z).astype(F32).astype(BF16)
    for k in range(ITERS - 1):
        a = jnp.where(at_row, res[0, k : k + 1, :], F32(0.0))
        hi, mid = split2(a)
        low = (a - hi.astype(F32) - mid.astype(F32)).astype(BF16)
        total = None
        for part in (low, mid, hi):
            d = lax.dot_general(
                part, at_z, (((1,), (1,)), ((), ())), preferred_element_type=F32
            )
            total = d if total is None else total + d
        RI[k] = total.reshape(nx, ny, nz)

    def zd(fields, forward):
        f = fields.reshape(-1, nz)
        hi, mid = split2(f)
        d = jnp.dot(
            jnp.concatenate([hi, mid], axis=1), MZ[int(forward)], preferred_element_type=F32
        )
        return (d[:, :nz] + d[:, nz:]).reshape(fields.shape)

    def yd(field, forward):
        hi, mid = split2(field.reshape(rows, nz))
        d = jnp.dot(
            MY[int(forward)], jnp.concatenate([hi, mid], axis=0), preferred_element_type=F32
        )
        return (d[:rows] + d[rows:]).reshape(nx, ny, nz)

    def xd(buf, w, comp, forward):
        total = None
        for m in range(1, 5):
            p, q = (m, 1 - m) if forward else (m - 1, -m)
            t = F32(TAPS[m - 1]) * (
                buf[w, comp, 4 + p : 4 + p + nx] - buf[w, comp, 4 + q : 4 + q + nx]
            )
            total = t if total is None else total + t
        return total

    def own(buf, w, comp):
        return buf[w, comp, 4 : 4 + nx]

    def local_strains(w):
        E[w, 1] = yd(own(V, w, 1), False)
        E[w, 2] = zd(own(V, w, 2), False)
        E[w, 3] = zd(own(V, w, 1), True) + yd(own(V, w, 2), True)
        E[w, 4] = zd(own(V, w, 0), True)
        E[w, 5] = yd(own(V, w, 0), True)

    def x_strains(w):
        E[w, 0] = xd(V, w, 0, False)
        E[w, 4] = E[w, 4] + xd(V, w, 2, True)
        E[w, 5] = E[w, 5] + xd(V, w, 1, True)

    def put(g, i, value, first):
        for p in range(shots):
            part = value[:, p * yp : (p + 1) * yp, :]
            g[p, i] = part if first else g[p, i] + part

    def image_local(first):
        put(GL, 0, E[0, 1] * E[1, 1], first)
        put(GL, 1, E[0, 2] * E[1, 2], first)
        put(GL, 2, E[0, 1] * E[1, 2] + E[0, 2] * E[1, 1], first)
        put(GL, 3, E[0, 3] * E[1, 3], first)
        put(
            GL, 4,
            own(V, 0, 0) * own(V, 1, 0) + own(V, 0, 1) * own(V, 1, 1)
            + own(V, 0, 2) * own(V, 1, 2),
            first,
        )

    def image_x(first):
        put(GX, 0, E[0, 0] * E[1, 0], first)
        put(GX, 1, E[0, 0] * E[1, 1] + E[0, 1] * E[1, 0], first)
        put(GX, 2, E[0, 0] * E[1, 2] + E[0, 2] * E[1, 0], first)
        put(GX, 3, E[0, 4] * E[1, 4], first)
        put(GX, 4, E[0, 5] * E[1, 5], first)

    def source_field(k):
        at = (
            lax.broadcasted_iota(jnp.int32, (nx, ny, nz), 0) * (ny * nz)
            + lax.broadcasted_iota(jnp.int32, (nx, ny, nz), 1) * nz
            + lax.broadcasted_iota(jnp.int32, (nx, ny, nz), 2)
        )
        return jnp.where(at == src[0] - dom * (rows * nz), wav[0, k], F32(0.0))

    def signed(w, base, change):
        return base + change if w else base - change

    def sums(g, landing, group):
        copies = []
        for o in range(1, shots):
            to = lax.rem(shot + o, shots)
            copies.append(
                pltpu.make_async_remote_copy(
                    src_ref=g.at[to],
                    dst_ref=landing.at[o - 1],
                    send_sem=gs_sem.at[group, o - 1],
                    recv_sem=gr_sem.at[group, o - 1],
                    device_id={"shot": to},
                    device_id_type=MESH,
                )
            )
        return copies

    loads[0].wait()
    loads[1].wait()
    for k in range(ITERS):
        for w in range(2):
            local_strains(w)
        if k == ITERS - 1:
            break
        if k == 0:
            for copy in loads[2:]:
                copy.wait()
        for w in range(2):
            wait_recv(2 * k, w)
            x_strains(w)
            if k:
                wait_send(2 * k - 1, w)
            exx, eyy, ezz = E[w, 0], E[w, 1], E[w, 2]
            sxx = signed(w, own(S, w, 0), C[0] * exx + C[3] * eyy + C[4] * ezz)
            if w == 0:
                sxx = sxx - source_field(k)
            S[w, 0, 4 : 4 + nx] = sxx
            S[w, 1, 4 : 4 + nx] = signed(w, own(S, w, 1), C[8] * E[w, 5])
            S[w, 2, 4 : 4 + nx] = signed(w, own(S, w, 2), C[7] * E[w, 4])
            send(2 * k + 1, w)
        for w in range(2):
            exx, eyy, ezz = E[w, 0], E[w, 1], E[w, 2]
            syy = signed(w, T[w, 0], C[3] * exx + C[1] * eyy + C[5] * ezz)
            szz = signed(w, T[w, 1], C[4] * exx + C[5] * eyy + C[2] * ezz)
            if w == 0:
                pulse = source_field(k)
                syy = syy - pulse
                szz = szz - pulse
            syz = signed(w, T[w, 2], C[6] * E[w, 3])
            T[w, 0] = syy
            T[w, 1] = szz
            T[w, 2] = syz
            Q[w, 0] = yd(own(S, w, 1), False) + zd(own(S, w, 2), False)
            Q[w, 1] = yd(syy, True) + zd(syz, False)
            Q[w, 2] = yd(syz, False) + zd(szz, True)
        image_local(k == 0)
        image_x(k == 0)
        for w in range(2):
            wait_recv(2 * k + 1, w)
            vx = signed(w, own(V, w, 0), B[...] * (xd(S, w, 0, True) + Q[w, 0]))
            vy = signed(w, own(V, w, 1), B[...] * (xd(S, w, 1, False) + Q[w, 1]))
            vz = signed(w, own(V, w, 2), B[...] * (xd(S, w, 2, False) + Q[w, 2]))
            if w:
                vz = vz + RI[k]
            if k:
                wait_send(2 * k, w)
            V[w, 0, 4 : 4 + nx] = vx
            V[w, 1, 4 : 4 + nx] = vy
            V[w, 2, 4 : 4 + nx] = vz
            send(2 * k + 2, w)

    image_local(False)
    for copy in sums(GL, RL, 0):
        copy.start()
    for w in range(2):
        wait_recv(2 * ITERS - 2, w)
        x_strains(w)
    image_x(False)
    for copy in sums(GX, RX, 1):
        copy.start()
    scale = F32(1.0 / ITERS)
    slots = ((1, 2, 5, 6, 9), (0, 3, 4, 7, 8))
    for group, (g, landing) in enumerate(((GL, RL), (GX, RX))):
        for copy in sums(g, landing, group):
            copy.wait_recv()
        for i, slot in enumerate(slots[group]):
            total = g[shot, i]
            for o in range(shots - 1):
                total = total + landing[o, i]
            out[slot] = total * scale
    for w in range(2):
        wait_send(0, w)
        wait_send(2 * ITERS - 3, w)
        wait_send(2 * ITERS - 2, w)
    for group, (g, landing) in enumerate(((GL, RL), (GX, RX))):
        for copy in sums(g, landing, group):
            copy.wait_send()


def body(shots, doms, fwd, adj, cn, cc, cs, buoy, wav, res, src, rcv):
    nx, ny, nz = buoy.shape
    field = (nx, ny, nz)
    yp = ny // shots
    wide = nx + 8
    stages = 2 * ITERS - 1
    hbm = pl.BlockSpec(memory_space=pl.ANY)
    vmem = pl.BlockSpec(memory_space=pltpu.VMEM)
    smem = pl.BlockSpec(memory_space=pltpu.SMEM)
    return pl.pallas_call(
        functools.partial(kernel, shots, doms),
        out_shape=jax.ShapeDtypeStruct((10, nx, yp, nz), F32),
        in_specs=[hbm] * 6 + [smem, vmem, smem, vmem],
        out_specs=vmem,
        scratch_shapes=[
            pltpu.VMEM((2, 3, wide, ny, nz), F32),
            pltpu.VMEM((2, 3, wide, ny, nz), F32),
            pltpu.VMEM((2, 3) + field, F32),
            pltpu.VMEM((9,) + field, F32),
            pltpu.VMEM(field, F32),
            pltpu.VMEM((2, 6) + field, F32),
            pltpu.VMEM((2, 3) + field, F32),
            pltpu.VMEM((ITERS - 1,) + field, F32),
            pltpu.VMEM((shots, 5, nx, yp, nz), F32),
            pltpu.VMEM((shots, 5, nx, yp, nz), F32),
            pltpu.VMEM((shots - 1, 5, nx, yp, nz), F32),
            pltpu.VMEM((shots - 1, 5, nx, yp, nz), F32),
            pltpu.VMEM((2, 2 * nz, 2 * nz), BF16),
            pltpu.VMEM((2, 2 * nx * ny, 2 * nx * ny), BF16),
            pltpu.SemaphoreType.DMA((14,)),
            pltpu.SemaphoreType.DMA((stages, 2, 2, 2)),
            pltpu.SemaphoreType.DMA((stages, 2, 2, 2)),
            pltpu.SemaphoreType.DMA((2, shots - 1)),
            pltpu.SemaphoreType.DMA((2, shots - 1)),
        ],
        compiler_params=pltpu.CompilerParams(
            collective_id=0, has_side_effects=True, vmem_limit_bytes=48 * 1024 * 1024
        ),
    )(fwd, adj, cn, cc, cs, buoy, wav, res, src, rcv)


def solution(mesh):
    placed = (
        P("shot", None, "dom", None, None),
        P("shot", None, "dom", None, None),
        P(None, "dom", None, None),
        P(None, "dom", None, None),
        P(None, "dom", None, None),
        P("dom", None, None),
        P("shot", None),
        P("shot", None, None),
        P("shot"),
        P("shot", None),
    )
    return jax.shard_map(
        functools.partial(body, mesh.shape["shot"], mesh.shape["dom"]),
        mesh=mesh,
        in_specs=placed,
        out_specs=P(None, "dom", "shot", None),
        check_vma=False,
    )
```

time: 129 us -> 41.6 us (0.32); the launches traced: 127 us -> 41 us
  waiting for transfers between devices: 43 us -> 0 us
  Pallas kernels: 0 us -> 33.2 us
  between operations: 27.6 us -> 0.69 us
  starting transfers between devices: 24.1 us -> 0 us
  other arithmetic: 24 us -> 0 us
    pallas_call x0 -> x1, Pallas kernels: none -> 33.2 us  [body(): pl.pallas_call(functools.partial(kernel, shots, doms), out_shape=jax.Shap...]
    ppermute x10 -> x0, waiting for transfers between devices: 26.7 us -> none  [the longest x5 21.7 us: padded_2(): lax.ppermute(head, axis, [((i + 1) % count, i) for i in range(ends)])]
    ppermute x10 -> x0, starting transfers between devices: 24.1 us -> none  [the longest x5 13 us: padded_2(): lax.ppermute(tail, axis, [(i, (i + 1) % count) for i in range(ends)])]
    reduce_scatter x1 -> x0, waiting for transfers between devices: 16.2 us -> none  [body(): lax.psum_scatter(running, 'shot', scatter_dimension=2, tiled=True)]
    add x23 -> x0, other arithmetic: 8.94 us -> none  [the longest x6 3.95 us: inject(): flattened = source.reshape(shot_count, volume).at[shot_ids, jnp.where(ins...]
    unnamed x31 -> x0, other arithmetic: 5.98 us -> none
    scatter-add x2 -> x0, other arithmetic: 4.62 us -> none  [inject(): flattened = source.reshape(shot_count, volume).at[shot_ids, jnp.where(ins...]
    another operation x10 -> x0, other arithmetic: 2.39 us -> none  [the longest x2 1.19 us: body(): paired = jnp.stack([fwd_state, adj_state], axis=1)]
  transfers between devices with their start and end apart: 11 -> 0, of which waited for: 9 -> 0; matrix products, arithmetic and copies ran while one was open for 2% -> 0% of each run, Pallas kernels for 0% -> 0%
where the time goes in v1:
time: 41.6 us; the launch traced here: 41 us
  Pallas kernels  33.2 us (80%)
  local copies, waits for them, and re-layouts  7.18 us (17%)
  between operations  0.69 us (2%)
    pallas_call x1, Pallas kernels, body(): pl.pallas_call(functools.partial(kernel, shots, doms), out_shape=jax.Shap...  33.2 us
    unnamed x18, local copies, waits for them, and re-layouts  7.18 us

profile of v1, /device:TPU:9, one launch (start us, length us, event | category | flops | bytes accessed | tf_op | source)
XLA Modules:
  0.0 41.0 jit_solution(7189405481509355364)
XLA Ops:
  0.7 0.0 copy-start.6
  0.7 0.0 copy-start.7
  0.7 0.7 %copy.11.res = f32[1,3,256]{2,1,0:T(4,128)S(1)} copy(f32[1,3,256]{2,0,1:T(1,128)} %param.17) | data formatting | bytes 6144 | tf_op args[7]
  1.4 0.0 copy-done.6
  1.4 0.0 copy-done.7
  1.4 0.0 copy-start
  1.4 1.1 %copy-done = f32[1,9,8,16,128]{4,3,2,1,0:T(8,128)S(1)} copy-done((f32[1,9,8,16,128]{4,3,2,1,0:T(8,128)S(1)}, f32[1,9,8,16,128]{4,3,2,1,0:T(8,128)}, u32[]{:S(2)}) %copy-start) | copy-done | bytes 589848
  2.4 0.0 copy-start.1
  2.4 1.1 %copy-done.1 = f32[1,9,8,16,128]{4,3,2,1,0:T(8,128)S(1)} copy-done((f32[1,9,8,16,128]{4,3,2,1,0:T(8,128)S(1)}, f32[1,9,8,16,128]{4,3,2,1,0:T(8,128)}, u32[]{:S(2)}) %copy-start.1) | copy-done | bytes 589848
  3.5 0.0 copy-start.2
  3.5 0.9 %copy-done.2 = f32[3,8,16,128]{3,2,1,0:T(8,128)S(1)} copy-done((f32[3,8,16,128]{3,2,1,0:T(8,128)S(1)}, f32[3,8,16,128]{3,2,1,0:T(8,128)}, u32[]{:S(2)}) %copy-start.2) | copy-done | bytes 196632
  4.4 0.0 copy-start.3
  4.4 0.9 %copy-done.3 = f32[3,8,16,128]{3,2,1,0:T(8,128)S(1)} copy-done((f32[3,8,16,128]{3,2,1,0:T(8,128)S(1)}, f32[3,8,16,128]{3,2,1,0:T(8,128)}, u32[]{:S(2)}) %copy-start.3) | copy-done | bytes 196632
  5.4 0.0 copy-start.4
  5.4 0.9 %copy-done.4 = f32[3,8,16,128]{3,2,1,0:T(8,128)S(1)} copy-done((f32[3,8,16,128]{3,2,1,0:T(8,128)S(1)}, f32[3,8,16,128]{3,2,1,0:T(8,128)}, u32[]{:S(2)}) %copy-start.4) | copy-done | bytes 196632
  6.3 0.0 copy-start.5
  6.3 0.8 %copy-done.5 = f32[8,16,128]{2,1,0:T(8,128)S(1)} copy-done((f32[8,16,128]{2,1,0:T(8,128)S(1)}, f32[8,16,128]{2,1,0:T(8,128)}, u32[]{:S(2)}) %copy-start.5) | copy-done | bytes 65560
  7.1 33.2 %shard_map.100 = f32[10,8,8,128]{3,2,1,0:T(8,128)S(1)} custom-call(f32[1,9,8,16,128]{4,3,2,1,0:T(8,128)S(1)} %copy-done, f32[1,9,8,16,128]{4,3,2,1,0:T(8,128)S(1)} %copy-done.1, f32[3,8,16,128]{3,2,1,0:T(8,128)S(1)} %copy-done.2, f32[3,8,16,128]{3,2,1,0:T(8,128)S(1)} %copy-done.3, f32[3,8,16,128]{3,2,1,0:T(8,128)S(1)} %copy-done.4, ...), custom_call_target="tpu_custom_call" | custom-call | tf_op jit(solution)/shard_map/pallas_call | solution.py:372
  40.3 0.7 %copy.14 = f32[10,8,8,128]{3,2,1,0:T(8,128)} copy(f32[10,8,8,128]{3,2,1,0:T(8,128)S(1)} %shard_map.100) | data formatting | bytes 655360
Async XLA Ops:
  0.7 0.7 %copy-start.6 = (s32[1,256]{1,0:T(1,128)S(1)}, s32[1,256]{1,0:T(1,128)}, u32[]{:S(2)}) copy-start(s32[1,256]{1,0:T(1,128)} %rcv.1) | copy-start | bytes 3076
  0.7 0.7 %copy-start.7 = (f32[1,3]{1,0:T(1,128)S(1)}, f32[1,3]{1,0:T(1,128)}, u32[]{:S(2)}) copy-start(f32[1,3]{1,0:T(1,128)} %wav.1) | copy-start | bytes 40
  1.4 1.1 %copy-start = (f32[1,9,8,16,128]{4,3,2,1,0:T(8,128)S(1)}, f32[1,9,8,16,128]{4,3,2,1,0:T(8,128)}, u32[]{:S(2)}) copy-start(f32[1,9,8,16,128]{4,3,2,1,0:T(8,128)} %fwd.1) | copy-start | bytes 1769476
  2.4 1.1 %copy-start.1 = (f32[1,9,8,16,128]{4,3,2,1,0:T(8,128)S(1)}, f32[1,9,8,16,128]{4,3,2,1,0:T(8,128)}, u32[]{:S(2)}) copy-start(f32[1,9,8,16,128]{4,3,2,1,0:T(8,128)} %adj.1) | copy-start | bytes 1769476
  3.5 0.9 %copy-start.2 = (f32[3,8,16,128]{3,2,1,0:T(8,128)S(1)}, f32[3,8,16,128]{3,2,1,0:T(8,128)}, u32[]{:S(2)}) copy-start(f32[3,8,16,128]{3,2,1,0:T(8,128)} %cn.1) | copy-start | bytes 589828
  4.4 0.9 %copy-start.3 = (f32[3,8,16,128]{3,2,1,0:T(8,128)S(1)}, f32[3,8,16,128]{3,2,1,0:T(8,128)}, u32[]{:S(2)}) copy-start(f32[3,8,16,128]{3,2,1,0:T(8,128)} %cc.1) | copy-start | bytes 589828
  5.4 0.9 %copy-start.4 = (f32[3,8,16,128]{3,2,1,0:T(8,128)S(1)}, f32[3,8,16,128]{3,2,1,0:T(8,128)}, u32[]{:S(2)}) copy-start(f32[3,8,16,128]{3,2,1,0:T(8,128)} %cs.1) | copy-start | bytes 589828
  6.3 0.8 %copy-start.5 = (f32[8,16,128]{2,1,0:T(8,128)S(1)}, f32[8,16,128]{2,1,0:T(8,128)}, u32[]{:S(2)}) copy-start(f32[8,16,128]{2,1,0:T(8,128)} %buoy.1) | copy-start | bytes 196612

commit v2 on v1

--- a/solution.py
+++ b/solution.py
@@ -13,10 +13,10 @@
 F32 = jnp.float32
 BF16 = jnp.bfloat16
 
-VEL_UP = ((slice(0, 1), 8, 0, 4), (slice(1, 3), 9, 1, 3))
-VEL_DOWN = ((slice(0, 1), 4, 12, 3), (slice(1, 3), 4, 12, 4))
-STR_UP = ((slice(0, 1), 9, 1, 3), (slice(1, 3), 8, 0, 4))
-STR_DOWN = ((slice(0, 1), 4, 12, 4), (slice(1, 3), 4, 12, 3))
+VEL_UP = ((slice(0, 1), 4), (slice(1, 3), 3))
+VEL_DOWN = ((slice(0, 1), 3), (slice(1, 3), 4))
+STR_UP = ((slice(0, 1), 3), (slice(1, 3), 4))
+STR_DOWN = ((slice(0, 1), 4), (slice(1, 3), 3))
 
 
 def split2(f):
@@ -38,7 +38,7 @@
     V, S, T, C, B, E, Q, RI, GL, GX, RL, RX, MZ, MY,
     load_sem, ssem, rsem, gs_sem, gr_sem,
 ):
-    nx, ny, nz = 8, V.shape[3], V.shape[4]
+    nx, ny, nz = B.shape
     rows = nx * ny
     yp = ny // shots
     dom = lax.axis_index("dom")
@@ -90,8 +90,8 @@
 
     @pl.when(jnp.logical_not(has_hi))
     def _():
-        V[:, :, 12:16] = jnp.zeros((2, 3, 4, ny, nz), F32)
-        S[:, :, 12:16] = jnp.zeros((2, 3, 4, ny, nz), F32)
+        V[:, :, 4 + nx : 8 + nx] = jnp.zeros((2, 3, 4, ny, nz), F32)
+        S[:, :, 4 + nx : 8 + nx] = jnp.zeros((2, 3, 4, ny, nz), F32)
 
     pl.semaphore_wait(
         barrier, has_lo.astype(jnp.int32) + has_hi.astype(jnp.int32) + (shots - 1)
@@ -101,7 +101,8 @@
         buf = S if stage % 2 else V
         plan = ((VEL_UP, VEL_DOWN), (STR_UP, STR_DOWN))[stage % 2][side]
         copies = []
-        for piece, (comp, at, to, count) in enumerate(plan):
+        for piece, (comp, count) in enumerate(plan):
+            at, to = (4, 4 + nx) if side else (4 + nx - count, 4 - count)
             if stage == 0:
                 source = states[w].at[0, comp, pl.ds(at - 4, count)]
             else:
@@ -170,13 +171,13 @@
 
     cell = rcv[...]
     local = cell - dom * (rows * nz)
-    cell_row = lax.shift_right_arithmetic(local, 7)
-    cell_z = jnp.bitwise_and(local, 127)
+    cell_row = local // nz
+    cell_z = local - nz * cell_row
     nrec = cell.shape[1]
     at_row = lax.broadcasted_iota(jnp.int32, (rows, nrec), 0) == cell_row
     at_z = (lax.broadcasted_iota(jnp.int32, (nz, nrec), 0) == cell_z).astype(F32).astype(BF16)
     for k in range(ITERS - 1):
-        a = jnp.where(at_row, res[0, k : k + 1, :], F32(0.0))
+        a = jnp.where(at_row, res[k], F32(0.0))
         hi, mid = split2(a)
         low = (a - hi.astype(F32) - mid.astype(F32)).astype(BF16)
         total = None
@@ -366,7 +367,7 @@
     yp = ny // shots
     wide = nx + 8
     stages = 2 * ITERS - 1
-    hbm = pl.BlockSpec(memory_space=pl.ANY)
+    hbm = pl.BlockSpec(memory_space=pltpu.HBM)
     vmem = pl.BlockSpec(memory_space=pltpu.VMEM)
     smem = pl.BlockSpec(memory_space=pltpu.SMEM)
     return pl.pallas_call(
@@ -396,9 +397,9 @@
             pltpu.SemaphoreType.DMA((2, shots - 1)),
         ],
         compiler_params=pltpu.CompilerParams(
-            collective_id=0, has_side_effects=True, vmem_limit_bytes=48 * 1024 * 1024
+            collective_id=0, has_side_effects=True, vmem_limit_bytes=63 * 1024 * 1024
         ),
-    )(fwd, adj, cn, cc, cs, buoy, wav, res, src, rcv)
+    )(fwd, adj, cn, cc, cs, buoy, wav, jnp.transpose(res, (1, 0, 2)), src, rcv)
 
 
 def solution(mesh):

time: 41.6 us -> 35 us (0.84)
  local copies, waits for them, and re-layouts: 7.18 us -> 1.72 us
  Pallas kernels: 33.2 us -> 32.3 us
    unnamed x18 -> x1, local copies, waits for them, and re-layouts: 7.18 us -> 1.72 us
    pallas_call x1, Pallas kernels: 33.2 us -> 32.3 us  [body(): pl.pallas_call(functools.partial(kernel, shots, doms), out_shape=jax.Shap...]
where the time goes in v2:
time: 35 us; the launch traced here: 34.6 us
  Pallas kernels  32.3 us (92%)
  local copies, waits for them, and re-layouts  1.72 us (5%)
  between operations  0.66 us (2%)
    pallas_call x1, Pallas kernels, body(): pl.pallas_call(functools.partial(kernel, shots, doms), out_shape=jax.Shap...  32.3 us
    unnamed x1, local copies, waits for them, and re-layouts  1.72 us

profile of v2, /device:TPU:9, one launch (start us, length us, event | category | flops | bytes accessed | tf_op | source)
XLA Modules:
  0.0 34.6 jit_solution(15443191509260992424)
XLA Ops:
  0.7 32.3 %shard_map.100 = f32[10,8,8,128]{3,2,1,0:T(8,128)} custom-call(f32[1,9,8,16,128]{4,3,2,1,0:T(8,128)} %fwd.1, f32[1,9,8,16,128]{4,3,2,1,0:T(8,128)} %adj.1, f32[3,8,16,128]{3,2,1,0:T(8,128)} %cn.1, f32[3,8,16,128]{3,2,1,0:T(8,128)} %cc.1, f32[3,8,16,128]{3,2,1,0:T(8,128)} %cs.1, f32[8,16,128]{2,1,0:T(8,128)} %buoy.1, f32[1,3]{1,0:T(1,128)} %wav.1, ...), custom_call_target="tpu_custom_call" | custom-call | tf_op jit(solution)/shard_map/pallas_call | solution.py:373
  32.9 1.7 %copy.13 = f32[10,8,8,128]{3,2,1,0:T(8,128)} copy(f32[10,8,8,128]{3,2,1,0:T(8,128)} %shard_map.100) | data formatting | bytes 655360

commit v3 on v2

--- a/solution.py
+++ b/solution.py
@@ -13,10 +13,8 @@
 F32 = jnp.float32
 BF16 = jnp.bfloat16
 
-VEL_UP = ((slice(0, 1), 4), (slice(1, 3), 3))
-VEL_DOWN = ((slice(0, 1), 3), (slice(1, 3), 4))
-STR_UP = ((slice(0, 1), 3), (slice(1, 3), 4))
-STR_DOWN = ((slice(0, 1), 4), (slice(1, 3), 3))
+VEL_LAYERS = ((4, 3, 3), (3, 4, 4))
+STR_LAYERS = ((3, 4, 4), (4, 3, 3))
 
 
 def split2(f):
@@ -97,63 +95,55 @@
         barrier, has_lo.astype(jnp.int32) + has_hi.astype(jnp.int32) + (shots - 1)
     )
 
-    def message(stage, w, side):
+    def message(stage, w, comp, side):
         buf = S if stage % 2 else V
-        plan = ((VEL_UP, VEL_DOWN), (STR_UP, STR_DOWN))[stage % 2][side]
-        copies = []
-        for piece, (comp, count) in enumerate(plan):
-            at, to = (4, 4 + nx) if side else (4 + nx - count, 4 - count)
-            if stage == 0:
-                source = states[w].at[0, comp, pl.ds(at - 4, count)]
-            else:
-                source = buf.at[w, comp, pl.ds(at, count)]
-            copies.append(
-                pltpu.make_async_remote_copy(
-                    src_ref=source,
-                    dst_ref=buf.at[w, comp, pl.ds(to, count)],
-                    send_sem=ssem.at[stage, w, side, piece],
-                    recv_sem=rsem.at[stage, w, side, piece],
-                    device_id={"dom": below if side else above},
-                    device_id_type=MESH,
-                )
-            )
-        return copies
-
-    def send(stage, w):
+        count = (VEL_LAYERS, STR_LAYERS)[stage % 2][side][comp]
+        at, to = (4, 4 + nx) if side else (4 + nx - count, 4 - count)
+        if stage == 0:
+            source = states[w].at[0, comp, pl.ds(at - 4, count)]
+        else:
+            source = buf.at[w, comp, pl.ds(at, count)]
+        return pltpu.make_async_remote_copy(
+            src_ref=source,
+            dst_ref=buf.at[w, comp, pl.ds(to, count)],
+            send_sem=ssem.at[stage, w, side, comp],
+            recv_sem=rsem.at[stage, w, side, comp],
+            device_id={"dom": below if side else above},
+            device_id_type=MESH,
+        )
+
+    def send(stage, w, comp):
         @pl.when(has_hi)
         def _():
-            for c in message(stage, w, 0):
-                c.start()
+            message(stage, w, comp, 0).start()
 
         @pl.when(has_lo)
         def _():
-            for c in message(stage, w, 1):
-                c.start()
-
-    def wait_send(stage, w):
+            message(stage, w, comp, 1).start()
+
+    def wait_send(stage, w, comps):
         @pl.when(has_hi)
         def _():
-            for c in message(stage, w, 0):
-                c.wait_send()
+            for comp in comps:
+                message(stage, w, comp, 0).wait_send()
 
         @pl.when(has_lo)
         def _():
-            for c in message(stage, w, 1):
-                c.wait_send()
-
-    def wait_recv(stage, w):
+            for comp in comps:
+                message(stage, w, comp, 1).wait_send()
+
+    def wait_recv(stage, w, comp):
         @pl.when(has_lo)
         def _():
-            for c in message(stage, w, 0):
-                c.wait_recv()
+            message(stage, w, comp, 0).wait_recv()
 
         @pl.when(has_hi)
         def _():
-            for c in message(stage, w, 1):
-                c.wait_recv()
+            message(stage, w, comp, 1).wait_recv()
 
     for w in range(2):
-        send(0, w)
+        for comp in range(3):
+            send(0, w, comp)
 
     r = lax.broadcasted_iota(jnp.int32, (nz, nz), 0)
     c = lax.broadcasted_iota(jnp.int32, (nz, nz), 1)
@@ -223,10 +213,12 @@
         E[w, 4] = zd(own(V, w, 0), True)
         E[w, 5] = yd(own(V, w, 0), True)
 
-    def x_strains(w):
-        E[w, 0] = xd(V, w, 0, False)
-        E[w, 4] = E[w, 4] + xd(V, w, 2, True)
-        E[w, 5] = E[w, 5] + xd(V, w, 1, True)
+    def x_strain(w, comp):
+        if comp == 0:
+            E[w, 0] = xd(V, w, 0, False)
+        else:
+            at = 6 - comp
+            E[w, at] = E[w, at] + xd(V, w, comp, True)
 
     def put(g, i, value, first):
         for p in range(shots):
@@ -245,10 +237,12 @@
             first,
         )
 
-    def image_x(first):
+    def image_xx(first):
         put(GX, 0, E[0, 0] * E[1, 0], first)
         put(GX, 1, E[0, 0] * E[1, 1] + E[0, 1] * E[1, 0], first)
         put(GX, 2, E[0, 0] * E[1, 2] + E[0, 2] * E[1, 0], first)
+
+    def image_shear(first):
         put(GX, 3, E[0, 4] * E[1, 4], first)
         put(GX, 4, E[0, 5] * E[1, 5], first)
 
@@ -263,14 +257,17 @@
     def signed(w, base, change):
         return base + change if w else base - change
 
-    def sums(g, landing, group):
+    groups = ((GL, RL, 0, 5), (GX, RX, 0, 3), (GX, RX, 3, 2))
+
+    def sums(group):
+        g, landing, at, count = groups[group]
         copies = []
         for o in range(1, shots):
             to = lax.rem(shot + o, shots)
             copies.append(
                 pltpu.make_async_remote_copy(
-                    src_ref=g.at[to],
-                    dst_ref=landing.at[o - 1],
+                    src_ref=g.at[to, pl.ds(at, count)],
+                    dst_ref=landing.at[o - 1, pl.ds(at, count)],
                     send_sem=gs_sem.at[group, o - 1],
                     recv_sem=gr_sem.at[group, o - 1],
                     device_id={"shot": to},
@@ -290,18 +287,20 @@
             for copy in loads[2:]:
                 copy.wait()
         for w in range(2):
-            wait_recv(2 * k, w)
-            x_strains(w)
-            if k:
-                wait_send(2 * k - 1, w)
-            exx, eyy, ezz = E[w, 0], E[w, 1], E[w, 2]
-            sxx = signed(w, own(S, w, 0), C[0] * exx + C[3] * eyy + C[4] * ezz)
-            if w == 0:
-                sxx = sxx - source_field(k)
-            S[w, 0, 4 : 4 + nx] = sxx
-            S[w, 1, 4 : 4 + nx] = signed(w, own(S, w, 1), C[8] * E[w, 5])
-            S[w, 2, 4 : 4 + nx] = signed(w, own(S, w, 2), C[7] * E[w, 4])
-            send(2 * k + 1, w)
+            for comp in range(3):
+                wait_recv(2 * k, w, comp)
+                x_strain(w, comp)
+                if k:
+                    wait_send(2 * k - 1, w, (comp,))
+                if comp == 0:
+                    change = C[0] * E[w, 0] + C[3] * E[w, 1] + C[4] * E[w, 2]
+                else:
+                    change = C[9 - comp] * E[w, 6 - comp]
+                stress = signed(w, own(S, w, comp), change)
+                if w == 0 and comp == 0:
+                    stress = stress - source_field(k)
+                S[w, comp, 4 : 4 + nx] = stress
+                send(2 * k + 1, w, comp)
         for w in range(2):
             exx, eyy, ezz = E[w, 0], E[w, 1], E[w, 2]
             syy = signed(w, T[w, 0], C[3] * exx + C[1] * eyy + C[5] * ezz)
@@ -318,46 +317,48 @@
             Q[w, 1] = yd(syy, True) + zd(syz, False)
             Q[w, 2] = yd(syz, False) + zd(szz, True)
         image_local(k == 0)
-        image_x(k == 0)
+        image_xx(k == 0)
+        image_shear(k == 0)
         for w in range(2):
-            wait_recv(2 * k + 1, w)
-            vx = signed(w, own(V, w, 0), B[...] * (xd(S, w, 0, True) + Q[w, 0]))
-            vy = signed(w, own(V, w, 1), B[...] * (xd(S, w, 1, False) + Q[w, 1]))
-            vz = signed(w, own(V, w, 2), B[...] * (xd(S, w, 2, False) + Q[w, 2]))
-            if w:
-                vz = vz + RI[k]
-            if k:
-                wait_send(2 * k, w)
-            V[w, 0, 4 : 4 + nx] = vx
-            V[w, 1, 4 : 4 + nx] = vy
-            V[w, 2, 4 : 4 + nx] = vz
-            send(2 * k + 2, w)
+            for comp in range(3):
+                wait_recv(2 * k + 1, w, comp)
+                change = B[...] * (xd(S, w, comp, comp == 0) + Q[w, comp])
+                velocity = signed(w, own(V, w, comp), change)
+                if w == 1 and comp == 2:
+                    velocity = velocity + RI[k]
+                if k:
+                    wait_send(2 * k, w, (comp,))
+                V[w, comp, 4 : 4 + nx] = velocity
+                send(2 * k + 2, w, comp)
 
     image_local(False)
-    for copy in sums(GL, RL, 0):
+    for copy in sums(0):
         copy.start()
-    for w in range(2):
-        wait_recv(2 * ITERS - 2, w)
-        x_strains(w)
-    image_x(False)
-    for copy in sums(GX, RX, 1):
+    for comp in range(3):
+        for w in range(2):
+            wait_recv(2 * ITERS - 2, w, comp)
+            x_strain(w, comp)
+        if comp == 0:
+            image_xx(False)
+            for copy in sums(1):
+                copy.start()
+    image_shear(False)
+    for copy in sums(2):
         copy.start()
-    scale = F32(1.0 / ITERS)
-    slots = ((1, 2, 5, 6, 9), (0, 3, 4, 7, 8))
-    for group, (g, landing) in enumerate(((GL, RL), (GX, RX))):
-        for copy in sums(g, landing, group):
+    slots = ((1, 2, 5, 6, 9), (0, 3, 4), (7, 8))
+    for group, (g, landing, at, count) in enumerate(groups):
+        for copy in sums(group):
             copy.wait_recv()
         for i, slot in enumerate(slots[group]):
-            total = g[shot, i]
+            total = g[shot, at + i]
             for o in range(shots - 1):
-                total = total + landing[o, i]
-            out[slot] = total * scale
+                total = total + landing[o, at + i]
+            out[slot] = total
     for w in range(2):
-        wait_send(0, w)
-        wait_send(2 * ITERS - 3, w)
-        wait_send(2 * ITERS - 2, w)
-    for group, (g, landing) in enumerate(((GL, RL), (GX, RX))):
-        for copy in sums(g, landing, group):
+        for stage in (0, 2 * ITERS - 3, 2 * ITERS - 2):
+            wait_send(stage, w, range(3))
+    for group in range(3):
+        for copy in sums(group):
             copy.wait_send()
 
 
@@ -370,7 +371,7 @@
     hbm = pl.BlockSpec(memory_space=pltpu.HBM)
     vmem = pl.BlockSpec(memory_space=pltpu.VMEM)
     smem = pl.BlockSpec(memory_space=pltpu.SMEM)
-    return pl.pallas_call(
+    summed = pl.pallas_call(
         functools.partial(kernel, shots, doms),
         out_shape=jax.ShapeDtypeStruct((10, nx, yp, nz), F32),
         in_specs=[hbm] * 6 + [smem, vmem, smem, vmem],
@@ -391,15 +392,16 @@
             pltpu.VMEM((2, 2 * nz, 2 * nz), BF16),
             pltpu.VMEM((2, 2 * nx * ny, 2 * nx * ny), BF16),
             pltpu.SemaphoreType.DMA((14,)),
-            pltpu.SemaphoreType.DMA((stages, 2, 2, 2)),
-            pltpu.SemaphoreType.DMA((stages, 2, 2, 2)),
-            pltpu.SemaphoreType.DMA((2, shots - 1)),
-            pltpu.SemaphoreType.DMA((2, shots - 1)),
+            pltpu.SemaphoreType.DMA((stages, 2, 2, 3)),
+            pltpu.SemaphoreType.DMA((stages, 2, 2, 3)),
+            pltpu.SemaphoreType.DMA((3, shots - 1)),
+            pltpu.SemaphoreType.DMA((3, shots - 1)),
         ],
         compiler_params=pltpu.CompilerParams(
             collective_id=0, has_side_effects=True, vmem_limit_bytes=63 * 1024 * 1024
         ),
     )(fwd, adj, cn, cc, cs, buoy, wav, jnp.transpose(res, (1, 0, 2)), src, rcv)
+    return summed / ITERS
 
 
 def solution(mesh):

time: 35 us -> 34.2 us (0.977)
  other arithmetic: 0 us -> 1.73 us
  local copies, waits for them, and re-layouts: 1.72 us -> 0 us
  Pallas kernels: 32.3 us -> 31.6 us
    div x0 -> x1, other arithmetic: none -> 1.73 us  [body(): return summed / ITERS]
    unnamed x1 -> x0, local copies, waits for them, and re-layouts: 1.72 us -> none
    pallas_call x1, Pallas kernels: 32.3 us -> 31.6 us  [body(): pl.pallas_call(functools.partial(kernel, shots, doms), out_shape=jax.Shap...]
where the time goes in v3:
time: 34.2 us; the launch traced here: 34 us
  Pallas kernels  31.6 us (92%)
  other arithmetic  1.73 us (5%)
  between operations  0.66 us (2%)
    pallas_call x1, Pallas kernels, body(): pl.pallas_call(functools.partial(kernel, shots, doms), out_shape=jax.Shap...  31.6 us
    div x1, other arithmetic, body(): return summed / ITERS  1.73 us

profile of v3, /device:TPU:9, one launch (start us, length us, event | category | flops | bytes accessed | tf_op | source)
XLA Modules:
  0.0 34.0 jit_solution(11441716273334038071)
XLA Ops:
  0.7 31.6 %shard_map.100 = f32[10,8,8,128]{3,2,1,0:T(8,128)} custom-call(f32[1,9,8,16,128]{4,3,2,1,0:T(8,128)} %fwd.1, f32[1,9,8,16,128]{4,3,2,1,0:T(8,128)} %adj.1, f32[3,8,16,128]{3,2,1,0:T(8,128)} %cn.1, f32[3,8,16,128]{3,2,1,0:T(8,128)} %cc.1, f32[3,8,16,128]{3,2,1,0:T(8,128)} %cs.1, f32[8,16,128]{2,1,0:T(8,128)} %buoy.1, f32[1,3]{1,0:T(1,128)} %wav.1, ...), custom_call_target="tpu_custom_call" | custom-call | tf_op jit(solution)/shard_map/pallas_call | solution.py:374
  32.3 1.7 %broadcast_multiply_fusion = f32[10,8,8,128]{3,2,1,0:T(8,128)} fusion(f32[10,8,8,128]{3,2,1,0:T(8,128)} %shard_map.100), kind=kLoop, calls=%fused_computation | loop fusion | flops 81920 | bytes 655360 | tf_op jit(solution)/shard_map/div | solution.py:404
